TPU v7x, 32 devices: a whole 2x2x4 slice. The times are simulated.
32 devices in a mesh: rep: 8 (over y, x, core), shard: 4 (over z).
Axes of the slice: x: 2, y: 2, z: 4, core: 2. Of those that a mesh axis runs over, the one named last changes fastest.
Arguments:
- tokens: bfloat16 [4096, 4608], P(('rep', 'shard')), may hold values from -384 to 384
- key_cot: bfloat16 [4096, 1024], P(('rep', 'shard')), may hold values from -6 to 6
- norm_gain: float32 [4608], replicated, may hold values from 0.5 to 1.5
- key_weight: bfloat16 [4608, 1024], P('shard'), may hold values from -0.09375 to 0.09375
- codes_m: int32 [4608, 1024], P('shard'), may hold values from 0 to 255
- codes_v: int32 [4608, 1024], P('shard'), may hold values from 0 to 255
- scale_m: float32 [2304], P('shard'), may hold values from 19.2 to 192
- scale_v: float32 [2304], P('shard'), may hold values from 409.6 to 8192
- qmap_m: float32 [256], replicated, may hold values from -1 to 1, as said below
- qmap_v: float32 [256], replicated, may hold values from 0.01 to 1, as said below
Outputs:
- input_grad: bfloat16 [4096, 4608], P(('rep', 'shard'))
- gain_grad: float32 [4608], replicated
- new_weight: bfloat16 [4608, 1024], P('shard')
- new_scale_m: float32 [2304], P('shard')
- new_scale_v: float32 [2304], P('shard')
Inputs may be any that keep to these rules, and one draw needn't show every extreme that they name: `qmap_m`: entries rise with the index. `qmap_v`: entries rise with the index.
All inputs are finite; a program needn't handle non-finite values.
Results may differ from a plain program's by a relative error of at most 0.0095.
Values may be sent and summed in bfloat16 or wider, within the bound.
A program may use at most 128 MiB of HBM per device.

v0:
```python
import math

import jax
import jax.numpy as jnp
from jax import lax
from jax.sharding import PartitionSpec as P

BLOCK = 2048


eps_norm = 1e-06
beta_one = 0.9
beta_two = 0.95
adam_eps = 1e-08
learn_rate = 0.01
decay_rate = 0.1
bias_one = 1.0 - 0.9**10
bias_two = 1.0 - 0.95**10


def normalize(tokens, norm_gain):
    wide = tokens.astype(jnp.float32)
    inv_rms = lax.rsqrt(jnp.mean(wide * wide, axis=-1, keepdims=True) + eps_norm)
    normed = (wide * inv_rms * norm_gain).astype(jnp.bfloat16)
    return (wide, inv_rms, normed)


def norm_backward(wide, inv_rms, norm_gain, normed_grad):
    scaled = normed_grad * norm_gain
    inner = jnp.mean(scaled * wide, axis=-1, keepdims=True)
    input_grad = (inv_rms * scaled - wide * inv_rms**3 * inner).astype(jnp.bfloat16)
    gain_term = jnp.sum(normed_grad * wide * inv_rms, axis=0)
    return (input_grad, gain_term)


def rounded(value):
    lowered = lax.optimization_barrier(value.astype(jnp.bfloat16))
    return lowered.astype(jnp.float32)


def decode(codes, table):
    high_part = codes // 16
    low_part = codes - high_part * 16
    levels = lax.broadcasted_iota(jnp.int32, (16, 1, 1), 0)
    pick_low = (low_part[None] == levels).astype(jnp.float32)
    pick_high = (high_part[None] == levels).astype(jnp.float32)
    table_grid = table.reshape(16, 16)
    by_high = jnp.einsum("hl,lrk->hrk", table_grid, pick_low, precision=lax.Precision.HIGHEST)
    return jnp.sum(pick_high * by_high, axis=0)


def adam_update(weight, grad, old_m, old_v):
    first = beta_one * old_m + (1.0 - beta_one) * grad
    second = beta_two * old_v + (1.0 - beta_two) * grad * grad
    direction = first / bias_one / (jnp.sqrt(second / bias_two) + adam_eps)
    new_weight = (
        weight.astype(jnp.float32) * (1.0 - learn_rate * decay_rate) - learn_rate * direction
    ).astype(jnp.bfloat16)
    return (new_weight, first, second)


def block_max(values, row_group):
    blocks = values.reshape(values.shape[0] // row_group, -1)
    return jnp.max(jnp.abs(blocks), axis=1)


def optimize(
    weight, grad, codes_first, codes_second, scales_first, scales_second, qmap_m, qmap_v, row_group
):
    rows, width = weight.shape
    span_rows = math.gcd(rows, 64)
    span_count = rows // span_rows
    per_span = span_rows // row_group

    def one_span(pieces):
        weight_part, grad_part, code_one, code_two, scale_one, scale_two = pieces
        old_m = (
            decode(code_one, qmap_m).reshape(per_span, row_group, width) * scale_one[:, None, None]
        ).reshape(span_rows, width)
        old_v = (
            decode(code_two, qmap_v).reshape(per_span, row_group, width) * scale_two[:, None, None]
        ).reshape(span_rows, width)
        new_part, first, second = adam_update(weight_part, grad_part, old_m, old_v)
        return (new_part, block_max(first, row_group), block_max(second, row_group))

    pieces = (
        weight.reshape(span_count, span_rows, width),
        grad.reshape(span_count, span_rows, width),
        codes_first.reshape(span_count, span_rows, width),
        codes_second.reshape(span_count, span_rows, width),
        scales_first.reshape(span_count, per_span),
        scales_second.reshape(span_count, per_span),
    )
    new_weight, new_first, new_second = lax.map(one_span, pieces)
    return (new_weight.reshape(rows, width), new_first.reshape(-1), new_second.reshape(-1))


def shards(
    tokens, key_cot, norm_gain, key_weight, codes_m, codes_v, scale_m, scale_v, qmap_m, qmap_v
):
    width = key_cot.shape[1]
    row_group = BLOCK // width
    wide, inv_rms, normed = normalize(tokens, norm_gain)
    group_cot = lax.all_gather(key_cot, "shard", axis=0, tiled=True)
    local_cols = jnp.einsum("tk,dk->td", group_cot, key_weight, preferred_element_type=jnp.float32)
    normed_grad = lax.all_to_all(local_cols, "shard", split_axis=0, concat_axis=1, tiled=True)
    input_grad, gain_term = norm_backward(wide, inv_rms, norm_gain, normed_grad)
    gain_grad = lax.psum(gain_term, ("rep", "shard"))
    shard_count = lax.axis_size("shard")
    rep_count = lax.axis_size("rep")
    slice_rows = key_weight.shape[0] // rep_count
    reordered = normed.reshape(normed.shape[0], shard_count, rep_count, slice_rows)
    reordered = reordered.transpose(0, 2, 1, 3).reshape(normed.shape)
    grad = lax.psum_scatter(
        rounded(jnp.einsum("td,tk->dk", reordered, key_cot, preferred_element_type=jnp.float32)),
        ("rep", "shard"),
        scatter_dimension=0,
        tiled=True,
    )
    first_row = lax.axis_index("rep") * slice_rows
    first_block = lax.axis_index("rep") * (slice_rows // row_group)

    def take_rows(array_in):
        return lax.dynamic_slice_in_dim(array_in, first_row, slice_rows, 0)

    def take_blocks(array_in):
        return lax.dynamic_slice_in_dim(array_in, first_block, slice_rows // row_group, 0)

    part_weight, part_m, part_v = optimize(
        take_rows(key_weight),
        grad,
        take_rows(codes_m),
        take_rows(codes_v),
        take_blocks(scale_m),
        take_blocks(scale_v),
        qmap_m,
        qmap_v,
        row_group,
    )
    new_weight = lax.all_gather(part_weight, "rep", axis=0, tiled=True)
    new_scale_m, new_scale_v = (
        lax.all_gather(part_m, "rep", axis=0, tiled=True),
        lax.all_gather(part_v, "rep", axis=0, tiled=True),
    )
    return (input_grad, gain_grad, new_weight, new_scale_m, new_scale_v)


def solution(mesh):
    placed = (
        P(("rep", "shard"), None),
        P(("rep", "shard"), None),
        P(),
        P("shard", None),
        P("shard", None),
        P("shard", None),
        P("shard"),
        P("shard"),
        P(),
        P(),
    )
    return jax.shard_map(
        shards,
        mesh=mesh,
        in_specs=placed,
        out_specs=(P(("rep", "shard"), None), P(), P("shard", None), P("shard"), P("shard")),
        check_vma=False,
    )
```

profile of v0, /device:TPU:0, one launch (start us, length us, event | category | flops | bytes accessed | tf_op | source)
XLA Modules:
  0.0 458.8 jit_solution(3579034933151415712)
XLA Ops:
  7.9 32.3 %all-gather.3.cloned.1.call-done = bf16[512,1024]{1,0:T(8,128)(2,1)} async-done(((bf16[128,1024]{1,0:T(8,128)(2,1)}), bf16[512,1024]{1,0:T(8,128)(2,1)}) %all-gather.3.cloned.1.call-update) | async-done | bytes 1048592 | tf_op jit(solution)/shard_map/all_gather | solution.py:104
  40.3 4.2 fusion.42
  44.4 4.5 all-to-all-start
  49.0 1.7 copy.16
  51.3 51.6 %all-to-all-done = f32[4,128,1152]{2,1,0:T(8,128)} async-done(((f32[4,128,1152]{2,1,0:T(8,128)}), f32[4,128,1152]{2,1,0:T(8,128)}, u32[]{:S(2)}, u32[]{:S(2)}) %all-to-all-start) | async-done | bytes 2359328 | tf_op jit(solution)/shard_map/all_to_all | solution.py:106
  103.0 3.0 copy.17
  106.0 4.4 fusion.39
  110.4 2.8 fusion.41
  114.2 5.1 %convolution_convert_fusion = bf16[4608,1024]{1,0:T(8,128)(2,1)} fusion(bf16[128,4608]{0,1:T(8,128)(2,1)S(1)} %bitcast.106, bf16[128,1024]{1,0:T(8,128)(2,1)S(1)} %copy-done.2), kind=kOutput, calls=%fused_computation.58 | convolution fusion | flops 1212678144 | bytes 10878976 | tf_op jit(solution)/shard_map/td,tk->dk/dot_general | solution.py:115
  119.3 12.7 %convert_element_type.39 = f32[4608,1024]{1,0:T(8,128)} convert(bf16[4608,1024]{1,0:T(8,128)(2,1)} %convolution_convert_fusion) | non-fusion elementwise | flops 4718592 | bytes 28311552 | tf_op jit(solution)/shard_map/convert_element_type | solution.py:38
  134.5 2.2 constant_dynamic-slice_fusion.2
  136.7 201.1 %reduce-scatter.2.cloned.1.call-done = f32[144,1024]{1,0:T(8,128)} async-done(((f32[4608,1024]{1,0:T(8,128)}), f32[144,1024]{1,0:T(8,128)}) %reduce-scatter.2.cloned.1.call-update) | async-done | bytes 589840 | tf_op jit(solution)/shard_map/reduce_scatter | solution.py:114
  337.8 53.6 %while.17 = (s32[]{:T(128)}, bf16[9,16,1024]{2,1,0:T(8,128)(2,1)}, f32[9,8]{1,0:T(8,128)S(1)}, f32[9,8]{1,0:T(8,128)S(1)}, bf16[9,16,1024]{2,1,0:T(8,128)(2,1)},...) while((s32[]{:T(128)}, bf16[9,16,1024]{2,1,0:T(8,128)(2,1)}, ...), condition=%wide.region_12.13_spmd, body=%wide.region_5.12_spmd.sunk | while | flops 103792624 | bytes 1253545 | solution.py:94
  340.7 1.0 fusion.64
  342.2 1.6 fusion.63
  348.1 1.6 fusion.63
  352.6 1.0 fusion.64
  354.1 1.6 fusion.63
  358.6 1.0 fusion.64
  360.1 1.6 fusion.63
  364.5 1.0 fusion.64
  366.0 1.6 fusion.63
  370.4 1.0 fusion.64
  372.0 1.6 fusion.63
  377.9 1.6 fusion.63
  382.4 1.0 fusion.64
  383.9 1.6 fusion.63
  389.8 1.6 fusion.63
  392.7 2.4 copy.19
  395.0 39.5 %psum.7 = f32[4608]{0:T(1024)} all-reduce(f32[4608]{0:T(1024)S(1)} %copy-done.3), channel_id=1, replica_groups=mesh['rep'=8,'shard'=4] {'rep','shard'}, use_global_device_ids=true, to_apply=%region_3.0 | all-reduce | flops 4608 | bytes 36864 | tf_op jit(solution)/shard_map/psum | solution.py:108
  435.2 13.8 %all-reduce.2 = (f32[576]{0:T(1024)}, f32[576]{0:T(1024)}) all-reduce(f32[576]{0:T(1024)S(1)} %dynamic-update-slice, f32[576]{0:T(1024)S(1)} %dynamic-update-slice.1), channel_id=1, replica_groups=mesh['rep'=8,'shard'=4] {'rep'}, use_global_device_ids=true, to_apply=%add | all-reduce | flops 1152 | bytes 9216
  449.0 3.3 copy.38
  (189 shorter events, 38.9 us)
Async XLA Ops:
  7.2 33.1 %copy-start = (bf16[1152,1024]{1,0:T(8,128)(2,1)S(1)}, bf16[1152,1024]{1,0:T(8,128)(2,1)}, u32[]{:S(2)}) copy-start(bf16[1152,1024]{1,0:T(8,128)(2,1)} %param.15) | copy-start | bytes 7077892
  7.2 33.1 %all-gather.3.cloned.1.call-start = ((), (), s32[]{:S(2)}) async-start(), calls=%async_computation.2 | async-start | bytes 1310720 | tf_op jit(solution)/shard_map/all_gather | solution.py:104
  44.4 58.5 %all-to-all-start = ((f32[4,128,1152]{2,1,0:T(8,128)}), f32[4,128,1152]{2,1,0:T(8,128)}, u32[]{:S(2)}, u32[]{:S(2)}) async-start(f32[4,128,1152]{2,1,0:T(8,128)} %bitcast.108), calls=%async_computation | async-start | bytes 4718592 | tf_op jit(solution)/shard_map/all_to_all | solution.py:106
  48.9 288.9 %reduce-scatter.2.cloned.1.call-start = ((), (), s32[]{:S(2)}) async-start(), calls=%async_computation.3 | async-start | bytes 19464192 | tf_op jit(solution)/shard_map/reduce_scatter | solution.py:114
  106.0 4.4 copy-start.1
  106.0 4.4 copy-start.4
  113.2 0.9 copy-start.2
  132.0 205.8 %copy-start.5 = (f32[256]{0:T(256)S(1)}, f32[256]{0:T(256)}, u32[]{:S(2)}) copy-start(f32[256]{0:T(256)} %param.20) | copy-start | bytes 3076
  132.0 205.8 %copy-start.6 = (f32[256]{0:T(256)S(1)}, f32[256]{0:T(256)}, u32[]{:S(2)}) copy-start(f32[256]{0:T(256)} %param.21) | copy-start | bytes 3076
  132.0 317.0 %all-gather.5.cloned.1.call-start = ((), (), s32[]{:S(2)}) async-start(), calls=%async_computation.4 | async-start | bytes 2654208 | tf_op jit(solution)/shard_map/all_gather | solution.py:140
  337.8 53.6 %copy-start.7 = (u32[32]{0:T(128)S(1)}, u32[32]{0:T(128)}, u32[]{:S(2)}) copy-start(u32[32]{0:T(128)} %constant.176) | copy-start | bytes 388
  391.4 3.7 copy-start.3
Sparse Core Ops, SparseCore 0:
  9.6 30.6 all-gather.2
  132.1 205.6 reduce-scatter.1
  391.5 28.0 all-gather.4
where the time goes:
time: 461 us; the launch traced here: 459 us
  waiting for transfers between devices  286 us (62%)
  other arithmetic  54.6 us (12%)
  blocking collectives  53.4 us (12%)
  local copies, waits for them, and re-layouts  23.4 us (5%)
  matrix products  22.2 us (5%)
  between operations  14.5 us (3%)
  starting transfers between devices  4.61 us (1%)
    reduce_scatter x1, waiting for transfers between devices, shards(): lax.psum_scatter(rounded(jnp.einsum('td,tk->dk', reordered, key_cot, pref...  201 us
    all_to_all x1, waiting for transfers between devices, shards(): lax.all_to_all(local_cols, 'shard', split_axis=0, concat_axis=1, tiled=True)  51.6 us
    psum x1, blocking collectives, shards(): gain_grad = lax.psum(gain_term, ('rep', 'shard'))  39.5 us
    all_gather x1, waiting for transfers between devices, shards(): group_cot = lax.all_gather(key_cot, 'shard', axis=0, tiled=True)  32.3 us
    dynamic_update_slice x9, other arithmetic, optimize(): new_weight, new_first, new_second = lax.map(one_span, pieces)  14.2 us
    unnamed x1, blocking collectives  13.8 us
    dot_general x18, matrix products, decode(): jnp.einsum('hl,lrk->hrk', table_grid, pick_low, precision=lax.Precision.H...  12.9 us
    convert_element_type x1, other arithmetic, rounded(): return lowered.astype(jnp.float32)  12.7 us
  transfers between devices with their start and end apart: 4, of which 3 were waited for; matrix products, arithmetic and copies ran while one was open for 2% of the time, Pallas kernels for 0%

commit v1 on v0

--- a/solution.py
+++ b/solution.py
@@ -3,6 +3,8 @@
 import jax
 import jax.numpy as jnp
 from jax import lax
+from jax.experimental import pallas as pl
+from jax.experimental.pallas import tpu as pltpu
 from jax.sharding import PartitionSpec as P
 
 BLOCK = 2048
@@ -95,7 +97,7 @@
     return (new_weight.reshape(rows, width), new_first.reshape(-1), new_second.reshape(-1))
 
 
-def shards(
+def plain_shards(
     tokens, key_cot, norm_gain, key_weight, codes_m, codes_v, scale_m, scale_v, qmap_m, qmap_v
 ):
     width = key_cot.shape[1]
@@ -145,6 +147,110 @@
     return (input_grad, gain_grad, new_weight, new_scale_m, new_scale_v)
 
 
+def lookup(codes, table):
+    low = codes & 127
+    first = jnp.take_along_axis(table[0], low, axis=1)
+    second = jnp.take_along_axis(table[1], low, axis=1)
+    return jnp.where(codes >= 128, second, first)
+
+
+def decode_kernel(rows, qm_ref, qv_ref, sm_ref, sv_ref, cm_hbm, cv_hbm, old_m, old_v, cm, cv, sems):
+    start = pl.multiple_of(lax.axis_index("rep") * rows, 8)
+    copies = [
+        pltpu.make_async_copy(src.at[pl.ds(start, rows)], dst, sems.at[i])
+        for i, (src, dst) in enumerate(((cm_hbm, cm), (cv_hbm, cv)))
+    ]
+    for copy in copies:
+        copy.start()
+    for copy, codes, table_ref, scale, out in (
+        (copies[0], cm, qm_ref, sm_ref, old_m),
+        (copies[1], cv, qv_ref, sv_ref, old_v),
+    ):
+        copy.wait()
+        tables = [jnp.broadcast_to(table_ref[i : i + 1, :], (8, 128)) for i in range(2)]
+
+        @pl.loop(0, rows // 8)
+        def _(step):
+            row = pl.multiple_of(step * 8, 8)
+            factor = scale[pl.ds(row, 8), :]
+            for col in range(0, codes.shape[1], 128):
+                value = lookup(codes[pl.ds(row, 8), col : col + 128], tables)
+                out[pl.ds(row, 8), col : col + 128] = value * factor
+
+
+def decode_rows(codes_m, codes_v, scale_m, scale_v, qmap_m, qmap_v, rows, row_group):
+    width = codes_m.shape[1]
+    first_block = lax.axis_index("rep") * (rows // row_group)
+
+    def spread(scale):
+        mine = lax.dynamic_slice_in_dim(scale, first_block, rows // row_group, 0)
+        return jnp.broadcast_to(jnp.repeat(mine, row_group)[:, None], (rows, 128))
+
+    vmem = pl.BlockSpec(memory_space=pltpu.VMEM)
+    anywhere = pl.BlockSpec(memory_space=pl.ANY)
+    shape = jax.ShapeDtypeStruct((rows, width), jnp.float32)
+    return pl.pallas_call(
+        lambda *refs: decode_kernel(rows, *refs),
+        out_shape=(shape, shape),
+        in_specs=[vmem] * 4 + [anywhere] * 2,
+        out_specs=(vmem, vmem),
+        scratch_shapes=[
+            pltpu.VMEM((rows, width), jnp.int32),
+            pltpu.VMEM((rows, width), jnp.int32),
+            pltpu.SemaphoreType.DMA((2,)),
+        ],
+        compiler_params=pltpu.CompilerParams(vmem_limit_bytes=16 * 2**20),
+        name="decode",
+    )(qmap_m.reshape(2, 128), qmap_v.reshape(2, 128), spread(scale_m), spread(scale_v), codes_m, codes_v)
+
+
+def tiled_shards(
+    tokens, key_cot, norm_gain, key_weight, codes_m, codes_v, scale_m, scale_v, qmap_m, qmap_v
+):
+    row_group = BLOCK // key_cot.shape[1]
+    features = tokens.shape[1]
+    rows = key_weight.shape[0]
+    slice_rows = rows // lax.axis_size("rep")
+    rep, shard = lax.axis_index("rep"), lax.axis_index("shard")
+    old_m, old_v = decode_rows(
+        codes_m, codes_v, scale_m, scale_v, qmap_m, qmap_v, slice_rows, row_group
+    )
+    wide = tokens.astype(jnp.float32)
+    inv_rms = lax.rsqrt(jnp.mean(wide * wide, axis=-1, keepdims=True) + eps_norm)
+    scaled_cot = (key_cot.astype(jnp.float32) * inv_rms).astype(jnp.bfloat16)
+    group_cot = lax.all_gather(scaled_cot, "shard", axis=0, tiled=True)
+    group_tokens = lax.all_to_all(tokens, "shard", split_axis=1, concat_axis=0, tiled=True)
+    cols = jnp.einsum("tk,dk->td", group_cot, key_weight, preferred_element_type=jnp.float32)
+    home = lax.all_to_all(
+        cols.astype(jnp.bfloat16), "shard", split_axis=0, concat_axis=1, tiled=True
+    ).astype(jnp.float32)
+    gain_term = lax.psum(jnp.sum(cols * group_tokens.astype(jnp.float32), axis=0), "rep")
+    gain_grad = lax.all_gather(gain_term, "shard", axis=0, tiled=True)
+    scaled = home * norm_gain
+    inner = jnp.sum(scaled * wide, axis=-1, keepdims=True) * (1.0 / features)
+    input_grad = (scaled - wide * (inv_rms * inv_rms * inner)).astype(jnp.bfloat16)
+    my_gain = lax.dynamic_slice_in_dim(norm_gain, shard * rows, rows, 0)
+    partial = jnp.einsum(
+        "td,tk->dk", group_tokens, group_cot, preferred_element_type=jnp.float32
+    ) * my_gain[:, None]
+    grad = lax.psum_scatter(
+        partial.astype(jnp.bfloat16), "rep", scatter_dimension=0, tiled=True
+    ).astype(jnp.float32)
+    my_weight = lax.dynamic_slice_in_dim(key_weight, rep * slice_rows, slice_rows, 0)
+    part_weight, first, second = adam_update(my_weight, grad, old_m, old_v)
+    new_weight = lax.all_gather(part_weight, "rep", axis=0, tiled=True)
+    maxima = jnp.stack([block_max(first, row_group), block_max(second, row_group)])
+    maxima = lax.all_gather(maxima, "rep", axis=1, tiled=True)
+    return (input_grad, gain_grad, new_weight, maxima[0], maxima[1])
+
+
+def shards(tokens, key_cot, norm_gain, key_weight, *rest):
+    slice_rows = key_weight.shape[0] // lax.axis_size("rep")
+    even = slice_rows % 16 == 0 and key_weight.shape[0] % 128 == 0
+    body = tiled_shards if even else plain_shards
+    return body(tokens, key_cot, norm_gain, key_weight, *rest)
+
+
 def solution(mesh):
     placed = (
         P(("rep", "shard"), None),

time: 461 us -> 161 us (0.35)
  waiting for transfers between devices: 286 us -> 67.8 us
  other arithmetic: 54.6 us -> 6.4 us
  blocking collectives: 53.4 us -> 35.2 us
  matrix products: 22.2 us -> 6.65 us
  local copies, waits for them, and re-layouts: 23.4 us -> 16.3 us
  starting transfers between devices: 4.61 us -> 10.1 us
    reduce_scatter x1, waiting for transfers between devices: 201 us -> 24.5 us  [tiled_shards(): lax.psum_scatter(partial.astype(jnp.bfloat16), 'rep', scatter_dimension=0...]
    all_to_all x1 -> x2, waiting for transfers between devices: 51.6 us -> 0.01 us  [the longest x1 0.01 us: tiled_shards(): lax.all_to_all(tokens, 'shard', split_axis=1, concat_axis=0, tiled=True)]
    psum x1, blocking collectives: 39.5 us -> 13.2 us  [tiled_shards(): lax.psum(jnp.sum(cols * group_tokens.astype(jnp.float32), axis=0), 'rep')]
    all_gather x0 -> x2, blocking collectives: none -> 22 us  [the longest x1 13.2 us: tiled_shards(): gain_grad = lax.all_gather(gain_term, 'shard', axis=0, tiled=True)]
    dot_general x20 -> x2, matrix products: 22.2 us -> 6.65 us  [the longest x1 4.07 us: tiled_shards(): jnp.einsum('td,tk->dk', group_tokens, group_cot, preferred_element_type=j...]
    dynamic_update_slice x9 -> x0, other arithmetic: 14.2 us -> none  [optimize(): new_weight, new_first, new_second = lax.map(one_span, pieces)]
    unnamed x1 -> x0, blocking collectives: 13.8 us -> none
    convert_element_type x2, other arithmetic: 15.5 us -> 2.27 us  [the longest x1 1.45 us: tiled_shards(): (scaled - wide * (inv_rms * inv_rms * inner)).astype(jnp.bfloat16)]
  transfers between devices with their start and end apart: 4 -> 5, of which waited for: 3 -> 2; matrix products, arithmetic and copies ran while one was open for 2% -> 9% of each run, Pallas kernels for 0% -> 3%
where the time goes in v1:
time: 161 us; the launch traced here: 160 us
  waiting for transfers between devices  67.8 us (42%)
  blocking collectives  35.2 us (22%)
  local copies, waits for them, and re-layouts  16.3 us (10%)
  between operations  14 us (9%)
  starting transfers between devices  10.1 us (6%)
  matrix products  6.65 us (4%)
  other arithmetic  6.4 us (4%)
  Pallas kernels  4.1 us (3%)
    all_gather x1, waiting for transfers between devices, tiled_shards(): group_cot = lax.all_gather(scaled_cot, 'shard', axis=0, tiled=True)  43.2 us
    reduce_scatter x1, waiting for transfers between devices, tiled_shards(): lax.psum_scatter(partial.astype(jnp.bfloat16), 'rep', scatter_dimension=0...  24.5 us
    all_gather x1, blocking collectives, tiled_shards(): gain_grad = lax.all_gather(gain_term, 'shard', axis=0, tiled=True)  13.2 us
    psum x1, blocking collectives, tiled_shards(): lax.psum(jnp.sum(cols * group_tokens.astype(jnp.float32), axis=0), 'rep')  13.2 us
    unnamed x30, local copies, waits for them, and re-layouts  9.83 us
    all_gather x1, blocking collectives, tiled_shards(): maxima = lax.all_gather(maxima, 'rep', axis=1, tiled=True)  8.85 us
    all_to_all x1, starting transfers between devices, tiled_shards(): lax.all_to_all(tokens, 'shard', split_axis=1, concat_axis=0, tiled=True)  6.45 us
    pallas_call x1, Pallas kernels, decode_rows(): pl.pallas_call(lambda *refs: decode_kernel(rows, *refs), out_shape=(shape...  4.1 us
  transfers between devices with their start and end apart: 5, of which 2 were waited for; matrix products, arithmetic and copies ran while one was open for 9% of the time, Pallas kernels for 3%

profile of v1, /device:TPU:0, one launch (start us, length us, event | category | flops | bytes accessed | tf_op | source)
XLA Modules:
  0.0 160.5 jit_solution(14795316893317828140)
XLA Ops:
  7.2 2.5 %copy.30 = bf16[16,4,8,1152]{3,2,0,1:T(8,128)(2,1)} copy(bf16[16,4,8,1152]{3,2,1,0:T(8,128)(2,1)} %bitcast.34) | data formatting | bytes 2359296 | tf_op jit(solution)/shard_map/all_to_all | solution.py:222
  9.7 6.4 %all-to-all-start.1 = ((bf16[128,4,1152]{2,0,1:T(8,128)(2,1)}), bf16[128,4,1152]{2,0,1:T(8,128)(2,1)S(1)}, u32[]{:S(2)}, u32[]{:S(2)}) async-start(bf16[128,4,1152]{2,0,1:T(8,128)(2,1)} %bitcast.29), calls=%async_computation.1 | async-start | bytes 2359296 | tf_op jit(solution)/shard_map/all_to_all | solution.py:222
  16.1 0.3 fusion.2
  16.4 0.5 copy-done.10
  16.9 0.8 multiply_convert_fusion
  17.8 0.8 dynamic_slice.15
  18.6 43.2 %all-gather.5.cloned.1.call-done = bf16[512,1024]{1,0:T(8,128)(2,1)} async-done(((bf16[128,1024]{1,0:T(8,128)(2,1)}), bf16[512,1024]{1,0:T(8,128)(2,1)}) %all-gather.5.cloned.1.call-update) | async-done | bytes 1048592 | tf_op jit(solution)/shard_map/all_gather | solution.py:221
  61.9 4.1 %fusion.1 = bf16[1152,1024]{1,0:T(8,128)(2,1)} fusion(bf16[512,1024]{1,0:T(8,128)(2,1)} %all-gather.5.cloned.1.call-done, bf16[512,1152]{1,0:T(8,128)(2,1)S(1)} %bitcast.35, f32[1152]{0:T(1024)S(1)} %dynamic_slice.15), kind=kOutput, calls=%fused_computation.5 | convolution fusion | flops 1210318848 | bytes 4592128 | tf_op jit(solution)/shard_map/td,tk->dk/dot_general | solution.py:233
  66.0 0.8 dynamic_slice.13
  66.8 0.1 broadcast_in_dim.25
  67.0 0.8 dynamic_slice.14
  67.8 0.1 broadcast_in_dim.28
  68.1 2.3 %copy-done = s32[1152,1024]{1,0:T(8,128)S(1)} copy-done((s32[1152,1024]{1,0:T(8,128)S(1)}, s32[1152,1024]{1,0:T(8,128)}, u32[]{:S(2)}) %copy-start) | copy-done | bytes 4718616
  70.5 2.5 %copy-done.1 = s32[1152,1024]{1,0:T(8,128)S(1)} copy-done((s32[1152,1024]{1,0:T(8,128)S(1)}, s32[1152,1024]{1,0:T(8,128)}, u32[]{:S(2)}) %copy-start.1) | copy-done | bytes 4718616
  73.0 4.1 %decode.1 = (f32[144,1024]{1,0:T(8,128)S(1)}, f32[144,1024]{1,0:T(8,128)S(1)}) custom-call(f32[2,128]{1,0:T(2,128)S(1)} %bitcast.30, f32[2,128]{1,0:T(2,128)S(1)} %bitcast.31, f32[144,128]{1,0:T(8,128)S(1)} %broadcast_in_dim.26.refs_2_, f32[144,128]{1,0:T(8,128)S(1)} %broadcast_in_dim.29.refs_3_, s32[1152,1024]{1,0:T(8,128)S(1)} %copy-done, ...), custom_call_target="tpu_custom_call" | custom-call | tf_op jit(solution)/shard_map/decode/pallas_call | solution.py:192
  77.1 2.6 %multiply_reduce_fusion = (f32[1152]{0:T(1024)S(1)}, bf16[512,1152]{1,0:T(8,128)(2,1)}) fusion(bf16[128,4,1152]{2,0,1:T(8,128)(2,1)S(1)} %all-to-all-done.1, bf16[512,1024]{1,0:T(8,128)(2,1)S(1)} %copy-done.12, bf16[1152,1024]{1,0:T(8,128)(2,1)S(1)} %copy-done.7), kind=kOutput, calls=%fused_computation.11 | convolution fusion | flops 1210317696 | bytes 5771776 | tf_op jit(solution)/shard_map/tk,dk->td/dot_general | solution.py:223
  79.7 3.5 %all-to-all-start = ((bf16[4,128,1152]{2,1,0:T(8,128)(2,1)}), bf16[4,128,1152]{2,1,0:T(8,128)(2,1)S(1)}, u32[]{:S(2)}, u32[]{:S(2)}) async-start(bf16[4,128,1152]{2,1,0:T(8,128)(2,1)} %bitcast.36), calls=%async_computation | async-start | bytes 2359296 | tf_op jit(solution)/shard_map/all_to_all | solution.py:224
  83.3 24.5 %reduce-scatter.2.cloned.1.call-done = bf16[144,1024]{1,0:T(8,128)(2,1)} async-done(((bf16[1152,1024]{1,0:T(8,128)(2,1)}), bf16[144,1024]{1,0:T(8,128)(2,1)}) %reduce-scatter.2.cloned.1.call-update) | async-done | bytes 294928 | tf_op jit(solution)/shard_map/reduce_scatter | solution.py:236
  107.8 2.9 %abs_reduce_fusion.1 = (f32[144]{0:T(256)}, f32[144]{0:T(256)}, bf16[144,1024]{1,0:T(8,128)(2,1)}) fusion(bf16[144,1024]{1,0:T(8,128)(2,1)} %reduce-scatter.2.cloned.1.call-done, f32[144,1024]{1,0:T(8,128)S(1)} %get-tuple-element.7, f32[144,1024]{1,0:T(8,128)S(1)} %get-tuple-element.8, bf16[1152,1024]{1,0:T(8,128)(2,1)} %param.13, s32[]{:T(128)S(6)} %select_n.10), kind=kLoop, calls=%fused_computation.18 | loop fusion | flops 3096288 | bytes 2065540 | tf_op jit(solution)/shard_map/reduce_max | solution.py:66
  110.7 13.2 %psum.7 = f32[1152]{0:T(1024)S(1)} all-reduce(f32[1152]{0:T(1024)S(1)} %get-tuple-element.13), channel_id=1, replica_groups=mesh['rep'=8,'shard'=4] {'rep'}, use_global_device_ids=true, to_apply=%region_3.0 | all-reduce | flops 1152 | bytes 9216 | tf_op jit(solution)/shard_map/psum | solution.py:227
  123.9 13.2 %all-gather = f32[4,1,1152]{2,1,0:T(1,128)S(1)} all-gather(f32[1,1,1152]{2,1,0:T(1,128)S(1)} %reshape.53), channel_id=1, replica_groups=mesh['rep'=8,'shard'=4] {'shard'}, dimensions={0}, use_global_device_ids=true | all-gather | bytes 23040 | tf_op jit(solution)/shard_map/all_gather | solution.py:228
  137.1 0.6 reshape.54
  137.8 0.2 convert_bitcast_fusion
  137.9 0.2 copy.28
  138.2 0.5 copy-done.6
  138.7 0.4 fusion.3
  139.2 1.5 fusion.5
  140.6 0.1 reduce_max.36
  140.8 0.1 reduce_max.24
  141.1 8.8 %all-gather.1 = f32[8,72,2]{1,2,0:T(2,128)S(1)} all-gather(f32[1,72,2]{1,2,0:T(2,128)S(1)} %maximum_bitcast_fusion), channel_id=1, replica_groups=mesh['rep'=8,'shard'=4] {'rep'}, dimensions={0}, use_global_device_ids=true | all-gather | bytes 5184 | tf_op jit(solution)/shard_map/all_gather | solution.py:243
  150.1 0.6 slice_reduce_fusion
  150.7 3.3 %copy.32 = bf16[1152,1024]{1,0:T(8,128)(2,1)} copy(bf16[1152,1024]{1,0:T(8,128)(2,1)} %all-gather.7.cloned.1.call-done) | data formatting | bytes 4718592
  (44 shorter events, 0.9 us)
Async XLA Ops:
  7.2 8.9 %copy-start.4 = (bf16[128,4608]{1,0:T(8,128)(2,1)S(1)}, bf16[128,4608]{1,0:T(8,128)(2,1)}, u32[]{:S(2)}) copy-start(bf16[128,4608]{1,0:T(8,128)(2,1)} %param.10) | copy-start | bytes 3538948
  9.6 7.3 %copy-start.5 = (bf16[128,1024]{1,0:T(8,128)(2,1)S(1)}, bf16[128,1024]{1,0:T(8,128)(2,1)}, u32[]{:S(2)}) copy-start(bf16[128,1024]{1,0:T(8,128)(2,1)} %param.11) | copy-start | bytes 786436
  9.7 52.2 %all-to-all-start.1 = ((bf16[128,4,1152]{2,0,1:T(8,128)(2,1)}), bf16[128,4,1152]{2,0,1:T(8,128)(2,1)S(1)}, u32[]{:S(2)}, u32[]{:S(2)}) async-start(bf16[128,4,1152]{2,0,1:T(8,128)(2,1)} %bitcast.29), calls=%async_computation.1 | async-start | bytes 2359296 | tf_op jit(solution)/shard_map/all_to_all | solution.py:222
  16.1 45.8 %all-gather.5.cloned.1.call-start = ((), (), s32[]{:S(2)}) async-start(), calls=%async_computation.3 | async-start | bytes 1310720 | tf_op jit(solution)/shard_map/all_gather | solution.py:221
  16.4 0.5 copy-start.10
  17.8 90.0 %reduce-scatter.2.cloned.1.call-start = ((), (), s32[]{:S(2)}) async-start(), calls=%async_computation.4 | async-start | bytes 2654208 | tf_op jit(solution)/shard_map/reduce_scatter | solution.py:236
  65.9 2.2 %copy-start.2 = (f32[256]{0:T(256)S(1)}, f32[256]{0:T(256)}, u32[]{:S(2)}) copy-start(f32[256]{0:T(256)} %param.18) | copy-start | bytes 3076
  65.9 2.2 %copy-start.3 = (f32[256]{0:T(256)S(1)}, f32[256]{0:T(256)}, u32[]{:S(2)}) copy-start(f32[256]{0:T(256)} %param.19) | copy-start | bytes 3076
  68.1 2.3 %copy-start = (s32[1152,1024]{1,0:T(8,128)S(1)}, s32[1152,1024]{1,0:T(8,128)}, u32[]{:S(2)}) copy-start(s32[1152,1024]{1,0:T(8,128)} %refs_4_.1) | copy-start | bytes 14155780
  70.5 2.5 %copy-start.1 = (s32[1152,1024]{1,0:T(8,128)S(1)}, s32[1152,1024]{1,0:T(8,128)}, u32[]{:S(2)}) copy-start(s32[1152,1024]{1,0:T(8,128)} %refs_5_.1) | copy-start | bytes 14155780
  73.0 4.1 %copy-start.7 = (bf16[1152,1024]{1,0:T(8,128)(2,1)S(1)}, bf16[1152,1024]{1,0:T(8,128)(2,1)}, u32[]{:S(2)}) copy-start(bf16[1152,1024]{1,0:T(8,128)(2,1)} %param.13) | copy-start | bytes 7077892
  73.0 4.1 %copy-start.12 = (bf16[512,1024]{1,0:T(8,128)(2,1)S(1)}, bf16[512,1024]{1,0:T(8,128)(2,1)}, u32[]{:S(2)}) copy-start(bf16[512,1024]{1,0:T(8,128)(2,1)} %all-gather.5.cloned.1.call-done) | copy-start | bytes 3145732
  79.7 58.1 %all-to-all-start = ((bf16[4,128,1152]{2,1,0:T(8,128)(2,1)}), bf16[4,128,1152]{2,1,0:T(8,128)(2,1)S(1)}, u32[]{:S(2)}, u32[]{:S(2)}) async-start(bf16[4,128,1152]{2,1,0:T(8,128)(2,1)} %bitcast.36), calls=%async_computation | async-start | bytes 2359296 | tf_op jit(solution)/shard_map/all_to_all | solution.py:224
  83.2 67.5 %all-gather.7.cloned.1.call-start = ((), (), s32[]{:S(2)}) async-start(), calls=%async_computation.5 | async-start | bytes 2654208 | tf_op jit(solution)/shard_map/all_gather | solution.py:241
  137.9 0.7 copy-start.6
  138.2 0.9 copy-start.11
  139.1 1.5 copy-start.9
  139.1 1.6 %copy-start.8 = (f32[144]{0:T(256)S(1)}, f32[144]{0:T(256)}, u32[]{:S(2)}) copy-start(f32[144]{0:T(256)} %get-tuple-element.9) | copy-start | bytes 1732
Sparse Core Ops, SparseCore 0:
  19.1 42.7 all-gather.4
  66.1 41.6 reduce-scatter.1
  110.8 29.0 all-gather.6

commit v2 on v0

--- a/solution.py
+++ b/solution.py
@@ -3,9 +3,13 @@
 import jax
 import jax.numpy as jnp
 from jax import lax
+from jax.experimental import pallas as pl
+from jax.experimental.pallas import tpu as pltpu
 from jax.sharding import PartitionSpec as P
 
 BLOCK = 2048
+CHUNKS = 3
+MESH = pl.DeviceIdType.MESH
 
 
 eps_norm = 1e-06
@@ -95,7 +99,7 @@
     return (new_weight.reshape(rows, width), new_first.reshape(-1), new_second.reshape(-1))
 
 
-def shards(
+def plain_shards(
     tokens, key_cot, norm_gain, key_weight, codes_m, codes_v, scale_m, scale_v, qmap_m, qmap_v
 ):
     width = key_cot.shape[1]
@@ -145,6 +149,514 @@
     return (input_grad, gain_grad, new_weight, new_scale_m, new_scale_v)
 
 
+def lookup(codes, table):
+    low = codes & 127
+    first = jnp.take_along_axis(table[0], low, axis=1)
+    second = jnp.take_along_axis(table[1], low, axis=1)
+    return jnp.where(codes >= 128, second, first)
+
+
+def decode_kernel(
+    chunks, chunk_rows, part, qm_ref, qv_ref, sm_ref, sv_ref, cm_hbm, cv_hbm, old_m, old_v, cm, cv, sems
+):
+    rows = chunks * part
+    copies = []
+    for i, (src, dst) in enumerate(((cm_hbm, cm), (cv_hbm, cv))):
+        for c in range(chunks):
+            start = pl.multiple_of(c * chunk_rows + lax.axis_index("rep") * part, 8)
+            copies.append(
+                pltpu.make_async_copy(
+                    src.at[pl.ds(start, part)], dst.at[pl.ds(c * part, part)], sems.at[i, c]
+                )
+            )
+    for copy in copies:
+        copy.start()
+    for waits, codes, table_ref, scale, out in (
+        (copies[:chunks], cm, qm_ref, sm_ref, old_m),
+        (copies[chunks:], cv, qv_ref, sv_ref, old_v),
+    ):
+        for copy in waits:
+            copy.wait()
+        tables = [jnp.broadcast_to(table_ref[i : i + 1, :], (8, 128)) for i in range(2)]
+
+        @pl.loop(0, rows // 8)
+        def _(step):
+            row = pl.multiple_of(step * 8, 8)
+            factor = scale[pl.ds(row, 8), :]
+            for col in range(0, codes.shape[1], 128):
+                value = lookup(codes[pl.ds(row, 8), col : col + 128], tables)
+                out[pl.ds(row, 8), col : col + 128] = value * factor
+
+
+def fused_kernel(
+    nr,
+    ns,
+    tok_hbm,
+    cot_ref,
+    gain_ref,
+    gain_rows,
+    w_hbm,
+    old_m,
+    old_v,
+    ig_ref,
+    nw_hbm,
+    gain_out,
+    scale_out,
+    tok_v,
+    w_v,
+    tok_g,
+    cot_g,
+    ng,
+    ng_home,
+    part,
+    core_recv,
+    red,
+    chip_recv,
+    nw_own,
+    inv_ref,
+    gain_own,
+    gain_recv,
+    gain_sum,
+    gain_z,
+    scale_own,
+    scale_recv,
+    loc,
+    cot_sem,
+    tok_sem,
+    ng_sem,
+    core_sem,
+    chip_sem,
+    ag_sem,
+    fwd_sem,
+    gain_sem,
+    gz_sem,
+    scale_sem,
+):
+    rep, shard = lax.axis_index("rep"), lax.axis_index("shard")
+    chips = nr // 2
+    chip, core = rep // 2, rep % 2
+    partner = rep + 1 - 2 * core
+    count, features = tok_v.shape
+    rows, width = w_v.shape
+    span = rows // CHUNKS
+    piece = span // nr
+    lanes = rows // 128
+
+    def remote(src, dst, sems, slot, **device):
+        return pltpu.make_async_remote_copy(
+            src_ref=src,
+            dst_ref=dst,
+            send_sem=sems.at[(0,) + slot],
+            recv_sem=sems.at[(1,) + slot],
+            device_id=device,
+            device_id_type=MESH,
+        )
+
+    def next_shard(k):
+        return lax.rem(shard + k, ns)
+
+    def next_rep(k):
+        return lax.rem(rep + k, nr)
+
+    def next_chip(k):
+        return lax.rem(chip + k, chips)
+
+    barrier = pltpu.get_barrier_semaphore()
+    for k in range(1, ns):
+        pl.semaphore_signal(barrier, inc=1, device_id={"shard": next_shard(k)}, device_id_type=MESH)
+    for k in range(1, nr):
+        pl.semaphore_signal(barrier, inc=1, device_id={"rep": next_rep(k)}, device_id_type=MESH)
+
+    load_tok = pltpu.make_async_copy(tok_hbm, tok_v, loc.at[0])
+    load_tok.start()
+    load_w = pltpu.make_async_copy(w_hbm, w_v, loc.at[1])
+    load_w.start()
+    mine = pl.ds(pl.multiple_of(shard * count, count), count)
+    own_tok = []
+    for c in range(CHUNKS):
+        col = pl.multiple_of(shard * rows + c * span, 128)
+        own_tok.append(
+            pltpu.make_async_copy(
+                tok_hbm.at[:, pl.ds(col, span)], tok_g.at[c, mine], loc.at[2 + c]
+            )
+        )
+        own_tok[c].start()
+    load_tok.wait()
+
+    @pl.loop(0, count // 16)
+    def _(step):
+        row = pl.multiple_of(step * 16, 16)
+        block = pl.ds(row, 16)
+        square = jnp.zeros((16, 128), jnp.float32)
+        for col in range(0, features, 128):
+            wide = tok_v[block, col : col + 128].astype(jnp.float32)
+            square = square + wide * wide
+        mean = jnp.sum(square, axis=1, keepdims=True) * (1.0 / features)
+        inv = lax.rsqrt(mean + eps_norm)
+        inv_ref[block, :] = jnp.broadcast_to(inv, (16, 128))
+        scaled = (cot_ref[block, :].astype(jnp.float32) * inv).astype(jnp.bfloat16)
+        cot_g[pl.ds(pl.multiple_of(shard * count + row, 16), 16), :] = scaled
+
+    pl.semaphore_wait(barrier, ns - 1 + nr - 1)
+
+    cot_copies = [
+        remote(cot_g.at[mine], cot_g.at[mine], cot_sem, (k - 1,), shard=next_shard(k))
+        for k in range(1, ns)
+    ]
+    for copy in cot_copies:
+        copy.start()
+    tok_copies = []
+    for c in range(CHUNKS):
+        for k in range(1, ns):
+            col = pl.multiple_of(next_shard(k) * rows + c * span, 128)
+            tok_copies.append(
+                remote(
+                    tok_hbm.at[:, pl.ds(col, span)],
+                    tok_g.at[c, mine],
+                    tok_sem,
+                    (c, k - 1),
+                    shard=next_shard(k),
+                )
+            )
+            tok_copies[-1].start()
+
+    load_w.wait()
+    for copy in cot_copies:
+        copy.wait_recv()
+
+    @pl.loop(0, CHUNKS)
+    def _(c):
+        rows_c = pl.ds(pl.multiple_of(c * span, 128), span)
+        ng[c] = lax.dot_general(
+            cot_g[...],
+            w_v[rows_c, :],
+            (((1,), (1,)), ((), ())),
+            preferred_element_type=jnp.float32,
+        ).astype(jnp.bfloat16)
+
+    own_ng = pltpu.make_async_copy(ng.at[:, mine], ng_home.at[shard], loc.at[2 + CHUNKS])
+    own_ng.start()
+    ng_copies = []
+    for k in range(1, ns):
+        theirs = pl.ds(pl.multiple_of(next_shard(k) * count, count), count)
+        ng_copies.append(
+            remote(ng.at[:, theirs], ng_home.at[shard], ng_sem, (k - 1,), shard=next_shard(k))
+        )
+
+    core_copies = [
+        remote(part.at[c, :, 1 - core], core_recv.at[c], core_sem, (c,), rep=partner)
+        for c in range(CHUNKS)
+    ]
+    chip_copies = [
+        [
+            remote(
+                red.at[c, next_chip(k)],
+                chip_recv.at[c, k - 1],
+                chip_sem,
+                (c, k - 1),
+                rep=next_chip(k) * 2 + core,
+            )
+            for k in range(1, chips)
+        ]
+        for c in range(CHUNKS)
+    ]
+
+    def out_rows(c, owner):
+        return pl.ds(pl.multiple_of(c * span + owner * piece, 16), piece)
+
+    ag_copies, fwd_copies, own_nw = [], [], []
+    for c in range(CHUNKS):
+        here = out_rows(c, rep)
+        targets = [next_chip(k) * 2 + core for k in range(1, chips)] + [partner]
+        ag_copies.append(
+            [
+                remote(nw_own.at[c], nw_hbm.at[here], ag_sem, (c, i), rep=target)
+                for i, target in enumerate(targets)
+            ]
+        )
+        own_nw.append(
+            pltpu.make_async_copy(nw_own.at[c], nw_hbm.at[here], loc.at[3 + CHUNKS + c])
+        )
+        steps = []
+        for k in range(1, chips):
+            there = out_rows(c, next_chip(chips - k) * 2 + core)
+            steps.append(
+                remote(nw_hbm.at[there], nw_hbm.at[there], fwd_sem, (c, k - 1), rep=partner)
+            )
+        fwd_copies.append(steps)
+
+    def form(c):
+        own_tok[c].wait()
+        for k in range(ns - 1):
+            tok_copies[c * (ns - 1) + k].wait_recv()
+        product = lax.dot_general(
+            tok_g[c], cot_g[...], (((0,), (0,)), ((), ())), preferred_element_type=jnp.float32
+        )
+        for j in range(nr):
+            part[c, j // 2, j % 2] = product[j * piece : (j + 1) * piece].astype(jnp.bfloat16)
+        core_copies[c].start()
+
+        def add(step, total):
+            block = pl.ds(pl.multiple_of(step * 32, 32), 32)
+            term = ng[c, block, :].astype(jnp.float32) * tok_g[c, block, :].astype(jnp.float32)
+            return total + term
+
+        total = lax.fori_loop(
+            0, ns * count // 32, add, jnp.zeros((32, span), jnp.float32)
+        )
+        line = jnp.sum(total, axis=0, keepdims=True)
+        for i in range(span // 128):
+            k = c * (span // 128) + i
+            gain_own[k : k + 1, :] = line[:, i * 128 : (i + 1) * 128]
+
+    def reduce_core(c):
+        core_copies[c].wait_recv()
+        for q in range(chips):
+            both = part[c, q, core].astype(jnp.float32) + core_recv[c, q].astype(jnp.float32)
+            red[c, q] = both.astype(jnp.bfloat16)
+        for copy in chip_copies[c]:
+            copy.start()
+
+    def update(c):
+        for copy in chip_copies[c]:
+            copy.wait_recv()
+        tops = [jnp.zeros((1, 128), jnp.float32)] * 2
+        for row in range(0, piece, 16):
+            block = slice(row, row + 16)
+            grad = red[c, chip, block, :].astype(jnp.float32)
+            for k in range(chips - 1):
+                grad = grad + chip_recv[c, k, block, :].astype(jnp.float32)
+            grad = grad * gain_rows[c, block, 0:1]
+            weight = w_v[pl.ds(pl.multiple_of(c * span + rep * piece + row, 16), 16), :]
+            new_part, first, second = adam_update(
+                weight, grad, old_m[c, block, :], old_v[c, block, :]
+            )
+            nw_own[c, block, :] = new_part
+            place = (
+                lax.broadcasted_iota(jnp.int32, (16, 128), 0)
+                + row
+                - 2 * lax.broadcasted_iota(jnp.int32, (16, 128), 1)
+            )
+            hit = (place == 0) | (place == 1)
+            for i, value in enumerate((jnp.abs(first), second)):
+                top = jnp.max(value, axis=1, keepdims=True)
+                spread = jnp.where(hit, jnp.broadcast_to(top, (16, 128)), 0.0)
+                tops[i] = jnp.maximum(tops[i], jnp.max(spread, axis=0, keepdims=True))
+        for copy in ag_copies[c]:
+            copy.start()
+        own_nw[c].start()
+        for i in range(2):
+            scale_own[2 * c + i : 2 * c + i + 1, :] = tops[i]
+
+    def forward(c):
+        for k in range(chips - 1):
+            ag_copies[c][k].wait_recv()
+            fwd_copies[c][k].start()
+
+    scale_own[...] = jnp.zeros_like(scale_own)
+    gain_own[...] = jnp.zeros_like(gain_own)
+    form(0)
+    reduce_core(0)
+    form(1)
+    reduce_core(1)
+    for copy in ng_copies:
+        copy.start()
+    update(0)
+    form(2)
+    gain_copies = [
+        remote(gain_own, gain_recv.at[k - 1], gain_sem, (k - 1,), rep=next_rep(k))
+        for k in range(1, nr)
+    ]
+    reduce_core(2)
+    for copy in gain_copies:
+        copy.start()
+    update(1)
+    forward(0)
+    update(2)
+    scale_copies = [
+        remote(scale_own, scale_recv.at[rep], scale_sem, (k - 1,), rep=next_rep(k))
+        for k in range(1, nr)
+    ]
+    for copy in scale_copies:
+        copy.start()
+    scale_recv[rep] = scale_own[...]
+    forward(1)
+    total = gain_own[...]
+    for k in range(nr - 1):
+        gain_copies[k].wait_recv()
+        total = total + gain_recv[k]
+    gain_sum[...] = total
+    gz_copies = [
+        remote(gain_sum, gain_z.at[shard], gz_sem, (k - 1,), shard=next_shard(k))
+        for k in range(1, ns)
+    ]
+    for copy in gz_copies:
+        copy.start()
+    gain_z[shard] = total
+    forward(2)
+
+    own_ng.wait()
+    for copy in ng_copies:
+        copy.wait_recv()
+
+    @pl.loop(0, count // 16)
+    def _(step):
+        block = pl.ds(pl.multiple_of(step * 16, 16), 16)
+        inner = jnp.zeros((16, 128), jnp.float32)
+        for col in range(0, features, 128):
+            p, c, o = col // rows, col % rows // span, col % span
+            scaled = ng_home[p, c, block, o : o + 128].astype(jnp.float32) * gain_ref[:, col : col + 128]
+            inner = inner + scaled * tok_v[block, col : col + 128].astype(jnp.float32)
+        inv = inv_ref[block, 0:1]
+        mean = jnp.sum(inner, axis=1, keepdims=True) * (1.0 / features)
+        factor = jnp.broadcast_to(inv * inv * mean, (16, 128))
+        for col in range(0, features, 128):
+            p, c, o = col // rows, col % rows // span, col % span
+            scaled = ng_home[p, c, block, o : o + 128].astype(jnp.float32) * gain_ref[:, col : col + 128]
+            wide = tok_v[block, col : col + 128].astype(jnp.float32)
+            ig_ref[block, col : col + 128] = (scaled - wide * factor).astype(jnp.bfloat16)
+
+    for copy in gz_copies + scale_copies:
+        copy.wait_recv()
+    gain_out[...] = gain_z[...]
+    scale_out[...] = scale_recv[...]
+    for c in range(CHUNKS):
+        own_nw[c].wait()
+        ag_copies[c][chips - 1].wait_recv()
+        for copy in fwd_copies[c]:
+            copy.wait_recv()
+            copy.wait_send()
+        for copy in ag_copies[c] + chip_copies[c]:
+            copy.wait_send()
+        core_copies[c].wait_send()
+    for copy in cot_copies + tok_copies + ng_copies + gain_copies + scale_copies + gz_copies:
+        copy.wait_send()
+
+
+def decode_rows(codes_m, codes_v, scale_m, scale_v, qmap_m, qmap_v, part, row_group):
+    width = codes_m.shape[1]
+    rows = CHUNKS * part
+
+    def spread(scale):
+        mine = scale.reshape(CHUNKS, -1, part // row_group)
+        mine = lax.dynamic_index_in_dim(mine, lax.axis_index("rep"), 1, keepdims=False)
+        return jnp.broadcast_to(jnp.repeat(mine.reshape(-1), row_group)[:, None], (rows, 128))
+
+    vmem = pl.BlockSpec(memory_space=pltpu.VMEM)
+    anywhere = pl.BlockSpec(memory_space=pl.ANY)
+    shape = jax.ShapeDtypeStruct((rows, width), jnp.float32)
+    chunk_rows = codes_m.shape[0] // CHUNKS
+    return pl.pallas_call(
+        lambda *refs: decode_kernel(CHUNKS, chunk_rows, part, *refs),
+        out_shape=(shape, shape),
+        in_specs=[vmem] * 4 + [anywhere] * 2,
+        out_specs=(vmem, vmem),
+        scratch_shapes=[
+            pltpu.VMEM((rows, width), jnp.int32),
+            pltpu.VMEM((rows, width), jnp.int32),
+            pltpu.SemaphoreType.DMA((2, CHUNKS)),
+        ],
+        compiler_params=pltpu.CompilerParams(vmem_limit_bytes=16 * 2**20),
+        name="decode",
+    )(qmap_m.reshape(2, 128), qmap_v.reshape(2, 128), spread(scale_m), spread(scale_v), codes_m, codes_v)
+
+
+def fused_shards(
+    tokens, key_cot, norm_gain, key_weight, codes_m, codes_v, scale_m, scale_v, qmap_m, qmap_v
+):
+    count, features = tokens.shape
+    rows, width = key_weight.shape
+    row_group = BLOCK // width
+    nr, ns = lax.axis_size("rep"), lax.axis_size("shard")
+    rep, shard = lax.axis_index("rep"), lax.axis_index("shard")
+    span = rows // CHUNKS
+    part = span // nr
+    chips = nr // 2
+    old_m, old_v = decode_rows(codes_m, codes_v, scale_m, scale_v, qmap_m, qmap_v, part, row_group)
+    gains = lax.dynamic_index_in_dim(norm_gain.reshape(ns, CHUNKS, nr, part), shard, 0, False)
+    gains = lax.dynamic_index_in_dim(gains, rep, 1, False)
+    gain_rows = jnp.broadcast_to(gains[:, :, None], (CHUNKS, part, 128))
+    vmem = pl.BlockSpec(memory_space=pltpu.VMEM)
+    anywhere = pl.BlockSpec(memory_space=pl.ANY)
+    lanes = -(-rows // 1024) * 8
+    levels = -(-2 * CHUNKS // 8) * 8
+    half, full = jnp.bfloat16, jnp.float32
+    dma = pltpu.SemaphoreType.DMA
+    input_grad, new_weight, gain_tiles, scale_tiles = pl.pallas_call(
+        lambda *refs: fused_kernel(nr, ns, *refs),
+        out_shape=(
+            jax.ShapeDtypeStruct((count, features), half),
+            jax.ShapeDtypeStruct((rows, width), half),
+            jax.ShapeDtypeStruct((ns, lanes, 128), full),
+            jax.ShapeDtypeStruct((nr, levels, 128), full),
+        ),
+        in_specs=[anywhere, vmem, vmem, vmem, anywhere, vmem, vmem],
+        out_specs=(vmem, anywhere, vmem, vmem),
+        scratch_shapes=[
+            pltpu.VMEM((count, features), half),
+            pltpu.VMEM((rows, width), half),
+            pltpu.VMEM((CHUNKS, ns * count, span), half),
+            pltpu.VMEM((ns * count, width), half),
+            pltpu.VMEM((CHUNKS, ns * count, span), half),
+            pltpu.VMEM((ns, CHUNKS, count, span), half),
+            pltpu.VMEM((CHUNKS, chips, 2, part, width), half),
+            pltpu.VMEM((CHUNKS, chips, part, width), half),
+            pltpu.VMEM((CHUNKS, chips, part, width), half),
+            pltpu.VMEM((CHUNKS, chips - 1, part, width), half),
+            pltpu.VMEM((CHUNKS, part, width), half),
+            pltpu.VMEM((count, 128), full),
+            pltpu.VMEM((lanes, 128), full),
+            pltpu.VMEM((nr - 1, lanes, 128), full),
+            pltpu.VMEM((lanes, 128), full),
+            pltpu.VMEM((ns, lanes, 128), full),
+            pltpu.VMEM((levels, 128), full),
+            pltpu.VMEM((nr, levels, 128), full),
+            dma((3 + 2 * CHUNKS,)),
+            dma((2, ns - 1)),
+            dma((2, CHUNKS, ns - 1)),
+            dma((2, ns - 1)),
+            dma((2, CHUNKS)),
+            dma((2, CHUNKS, chips - 1)),
+            dma((2, CHUNKS, chips)),
+            dma((2, CHUNKS, chips - 1)),
+            dma((2, nr - 1)),
+            dma((2, ns - 1)),
+            dma((2, nr - 1)),
+        ],
+        compiler_params=pltpu.CompilerParams(
+            collective_id=0, has_side_effects=True, vmem_limit_bytes=48 * 2**20
+        ),
+        cost_estimate=pl.CostEstimate(
+            flops=4 * ns * count * rows * width, bytes_accessed=12 * 2**20, transcendentals=0
+        ),
+        name="fused",
+    )(
+        tokens,
+        key_cot,
+        norm_gain.reshape(1, features),
+        gain_rows,
+        key_weight,
+        old_m.reshape(CHUNKS, part, width),
+        old_v.reshape(CHUNKS, part, width),
+    )
+    gain_grad = gain_tiles[:, : rows // 128].reshape(features)
+    maxima = scale_tiles[:, : 2 * CHUNKS, : part // row_group]
+    maxima = maxima.reshape(nr, CHUNKS, 2, part // row_group).transpose(2, 1, 0, 3).reshape(2, -1)
+    return (input_grad, gain_grad, new_weight, maxima[0], maxima[1])
+
+
+def shards(tokens, key_cot, norm_gain, key_weight, *rest):
+    part = key_weight.shape[0] // CHUNKS // lax.axis_size("rep")
+    even = (
+        key_weight.shape[0] % (CHUNKS * 128) == 0
+        and part % 16 == 0
+        and lax.axis_size("rep") % 2 == 0
+        and key_cot.shape[1] * 2 == BLOCK
+    )
+    body = fused_shards if even else plain_shards
+    return body(tokens, key_cot, norm_gain, key_weight, *rest)
+
+
 def solution(mesh):
     placed = (
         P(("rep", "shard"), None),

time: 461 us -> 108 us (0.23)
  the two profiles are of different devices: /device:TPU:0 before, /device:TPU:15 now
where the time goes in v2:
time: 108 us; the launch traced here: 107 us
  Pallas kernels  90.8 us (84%)
  local copies, waits for them, and re-layouts  15.8 us (15%)
    pallas_call x1, Pallas kernels, fused_shards(): pl.pallas_call(lambda *refs: fused_kernel(nr, ns, *refs), out_shape=(jax....  85.4 us
    unnamed x17, local copies, waits for them, and re-layouts  8.47 us
    pallas_call x1, Pallas kernels, decode_rows(): pl.pallas_call(lambda *refs: decode_kernel(CHUNKS, chunk_rows, part, *ref...  5.41 us
    squeeze x2, local copies, waits for them, and re-layouts, fused_shards(): return (input_grad, gain_grad, new_weight, maxima[0], maxima[1])  2.16 us

profile of v2, /device:TPU:15, one launch (start us, length us, event | category | flops | bytes accessed | tf_op | source)
XLA Modules:
  0.0 107.3 jit_solution(15249913024571723167)
XLA Ops:
  0.6 0.8 reshape.63
  1.4 0.8 reshape.65
  2.2 0.1 reshape.66
  2.3 0.1 reshape.64
  2.4 0.7 reshape.59.refs_2_
  3.1 0.1 broadcast_in_dim.30
  3.2 0.1 broadcast_in_dim.31
  3.3 0.1 broadcast_in_dim.33
  3.4 0.1 broadcast_in_dim.34
  3.6 0.8 reshape.60
  4.4 0.1 broadcast_in_dim.29.refs_3_
  4.5 0.1 broadcast_in_dim.35.refs_3_
  4.6 0.1 broadcast_in_dim.32.refs_2_
  4.7 0.0 copy-start
  4.7 2.3 %copy-done = s32[1152,1024]{1,0:T(8,128)S(1)} copy-done((s32[1152,1024]{1,0:T(8,128)S(1)}, s32[1152,1024]{1,0:T(8,128)}, u32[]{:S(2)}) %copy-start) | copy-done | bytes 4718616
  7.0 0.0 copy-start.1
  7.0 2.3 %copy-done.1 = s32[1152,1024]{1,0:T(8,128)S(1)} copy-done((s32[1152,1024]{1,0:T(8,128)S(1)}, s32[1152,1024]{1,0:T(8,128)}, u32[]{:S(2)}) %copy-start.1) | copy-done | bytes 4718616
  9.3 0.0 copy-start.2
  9.3 0.7 copy-done.2
  10.0 0.0 copy-start.3
  10.0 0.7 copy-done.3
  10.7 5.4 %decode.1 = (f32[144,1024]{1,0:T(8,128)S(1)}, f32[144,1024]{1,0:T(8,128)S(1)}) custom-call(f32[2,128]{1,0:T(2,128)S(1)} %bitcast.22, f32[2,128]{1,0:T(2,128)S(1)} %bitcast.23, f32[144,128]{1,0:T(8,128)S(1)} %broadcast_in_dim.32.refs_2_, f32[144,128]{1,0:T(8,128)S(1)} %broadcast_in_dim.35.refs_3_, s32[1152,1024]{1,0:T(8,128)S(1)} %copy-done, ...), custom_call_target="tpu_custom_call" | custom-call | tf_op jit(solution)/shard_map/decode/pallas_call | solution.py:549
  16.1 0.0 copy-done.4
  16.1 0.0 copy-done.5
  16.1 85.4 %fused.1 = (bf16[128,4608]{1,0:T(8,128)(2,1)S(1)}, bf16[1152,1024]{1,0:T(8,128)(2,1)}, f32[4,16,128]{2,1,0:T(8,128)S(1)}, f32[8,8,128]{2,1,0:T(8,128)S(1)}) custom-call(bf16[128,4608]{1,0:T(8,128)(2,1)S(1)} %copy-done.4, bf16[128,1024]{1,0:T(8,128)(2,1)S(1)} %copy-done.5, f32[1,4608]{1,0:T(1,128)S(1)} %reshape.59.refs_2_, ...), custom_call_target="tpu_custom_call" | custom-call | flops 2415919104 | bytes 12582912 | tf_op jit(solution)/shard_map/fused/pallas_call | solution.py:585
  101.5 0.6 reshape.69
  102.1 0.6 fusion
  102.7 1.5 %squeeze.14 = f32[576]{0:T(1024)} reshape(f32[1,3,8,24]{3,2,0,1:T(8,128)} %get-tuple-element.17) | data formatting | bytes 4608 | tf_op jit(solution)/shard_map/squeeze | solution.py:645
  104.2 0.7 squeeze.13
  104.9 1.0 copy.21
  105.9 0.0 copy-done.6
  105.9 1.4 %copy.22 = bf16[1152,1024]{1,0:T(8,128)(2,1)} copy(bf16[1152,1024]{1,0:T(8,128)(2,1)S(1)} %copy-done.6) | data formatting | bytes 4718592
  (7 shorter events, 0.1 us)
Async XLA Ops:
  4.7 2.4 %copy-start = (s32[1152,1024]{1,0:T(8,128)S(1)}, s32[1152,1024]{1,0:T(8,128)}, u32[]{:S(2)}) copy-start(s32[1152,1024]{1,0:T(8,128)} %refs_4_.2) | copy-start | bytes 14155780
  7.0 2.3 %copy-start.1 = (s32[1152,1024]{1,0:T(8,128)S(1)}, s32[1152,1024]{1,0:T(8,128)}, u32[]{:S(2)}) copy-start(s32[1152,1024]{1,0:T(8,128)} %refs_5_.1) | copy-start | bytes 14155780
  9.3 0.7 copy-start.2
  10.0 0.7 copy-start.3
  10.7 5.4 %copy-start.4 = (bf16[128,4608]{1,0:T(8,128)(2,1)S(1)}, bf16[128,4608]{1,0:T(8,128)(2,1)}, u32[]{:S(2)}) copy-start(bf16[128,4608]{1,0:T(8,128)(2,1)} %refs_0_.1) | copy-start | bytes 3538948
  10.7 5.4 %copy-start.5 = (bf16[128,1024]{1,0:T(8,128)(2,1)S(1)}, bf16[128,1024]{1,0:T(8,128)(2,1)}, u32[]{:S(2)}) copy-start(bf16[128,1024]{1,0:T(8,128)(2,1)} %refs_1_.1) | copy-start | bytes 786436
  102.1 3.8 %copy-start.6 = (bf16[1152,1024]{1,0:T(8,128)(2,1)S(1)}, bf16[1152,1024]{1,0:T(8,128)(2,1)}, u32[]{:S(2)}) copy-start(bf16[1152,1024]{1,0:T(8,128)(2,1)} %get-tuple-element.28) | copy-start | bytes 7077892

commit v3 on v2

--- a/solution.py
+++ b/solution.py
@@ -156,36 +156,12 @@
     return jnp.where(codes >= 128, second, first)
 
 
-def decode_kernel(
-    chunks, chunk_rows, part, qm_ref, qv_ref, sm_ref, sv_ref, cm_hbm, cv_hbm, old_m, old_v, cm, cv, sems
-):
-    rows = chunks * part
-    copies = []
-    for i, (src, dst) in enumerate(((cm_hbm, cm), (cv_hbm, cv))):
-        for c in range(chunks):
-            start = pl.multiple_of(c * chunk_rows + lax.axis_index("rep") * part, 8)
-            copies.append(
-                pltpu.make_async_copy(
-                    src.at[pl.ds(start, part)], dst.at[pl.ds(c * part, part)], sems.at[i, c]
-                )
-            )
-    for copy in copies:
-        copy.start()
-    for waits, codes, table_ref, scale, out in (
-        (copies[:chunks], cm, qm_ref, sm_ref, old_m),
-        (copies[chunks:], cv, qv_ref, sv_ref, old_v),
-    ):
-        for copy in waits:
-            copy.wait()
-        tables = [jnp.broadcast_to(table_ref[i : i + 1, :], (8, 128)) for i in range(2)]
-
-        @pl.loop(0, rows // 8)
-        def _(step):
-            row = pl.multiple_of(step * 8, 8)
-            factor = scale[pl.ds(row, 8), :]
-            for col in range(0, codes.shape[1], 128):
-                value = lookup(codes[pl.ds(row, 8), col : col + 128], tables)
-                out[pl.ds(row, 8), col : col + 128] = value * factor
+def column(values, first, repeat, count):
+    row = lax.broadcasted_iota(jnp.int32, (count, 128), 0)
+    out = jnp.full((count, 128), values[first], jnp.float32)
+    for i in range(1, count // repeat):
+        out = jnp.where(row >= i * repeat, values[first + i], out)
+    return out
 
 
 def fused_kernel(
@@ -194,10 +170,14 @@
     tok_hbm,
     cot_ref,
     gain_ref,
-    gain_rows,
+    gains,
     w_hbm,
-    old_m,
-    old_v,
+    codes_m,
+    codes_v,
+    scale_m,
+    scale_v,
+    table_m,
+    table_v,
     ig_ref,
     nw_hbm,
     gain_out,
@@ -220,6 +200,9 @@
     gain_z,
     scale_own,
     scale_recv,
+    held_codes,
+    old,
+    code_sem,
     loc,
     cot_sem,
     tok_sem,
@@ -271,6 +254,16 @@
     load_tok.start()
     load_w = pltpu.make_async_copy(w_hbm, w_v, loc.at[1])
     load_w.start()
+    loads = []
+    for i, codes in enumerate((codes_m, codes_v)):
+        for c in range(CHUNKS):
+            start = pl.multiple_of(c * span + rep * piece, 16)
+            loads.append(
+                pltpu.make_async_copy(
+                    codes.at[pl.ds(start, piece)], held_codes.at[i, c], code_sem.at[i, c]
+                )
+            )
+            loads[-1].start()
     mine = pl.ds(pl.multiple_of(shard * count, count), count)
     own_tok = []
     for c in range(CHUNKS):
@@ -299,12 +292,6 @@
 
     pl.semaphore_wait(barrier, ns - 1 + nr - 1)
 
-    cot_copies = [
-        remote(cot_g.at[mine], cot_g.at[mine], cot_sem, (k - 1,), shard=next_shard(k))
-        for k in range(1, ns)
-    ]
-    for copy in cot_copies:
-        copy.start()
     tok_copies = []
     for c in range(CHUNKS):
         for k in range(1, ns):
@@ -318,12 +305,70 @@
                     shard=next_shard(k),
                 )
             )
-            tok_copies[-1].start()
+
+    def send_tokens(c):
+        for k in range(ns - 1):
+            tok_copies[c * (ns - 1) + k].start()
+
+    def decode(i):
+        table_ref, scale = ((table_m, scale_m), (table_v, scale_v))[i]
+        tables = [jnp.broadcast_to(table_ref[k : k + 1, :], (8, 128)) for k in range(2)]
+        group = BLOCK // width
+        for c in range(CHUNKS):
+            loads[i * CHUNKS + c].wait()
+
+            @pl.loop(0, piece // 8)
+            def _(step):
+                block = pl.ds(pl.multiple_of(step * 8, 8), 8)
+                first = (c * span + rep * piece) // group + step * (8 // group)
+                factor = column(scale, first, group, 8)
+                for col in range(0, width, 128):
+                    value = lookup(held_codes[i, c, block, col : col + 128], tables)
+                    old[i, c, block, col : col + 128] = value * factor
+
+    def relay(way, t):
+        origin = jnp.clip(shard - way * t, 0, ns - 1)
+        block = cot_g.at[pl.ds(pl.multiple_of(origin * count, count), count)]
+        there = jnp.clip(shard + way, 0, ns - 1)
+        return remote(block, block, cot_sem, ((1 - way) // 2, t), shard=there)
+
+    def sends(way, t):
+        if way > 0:
+            return (shard + 1 < ns) & (shard >= t)
+        return (shard >= 1) & (shard + t < ns)
+
+    def takes(way, t):
+        return shard >= t + 1 if way > 0 else shard + t + 1 < ns
+
+    for t in range(ns - 1):
+        for way in (1, -1):
+            if t > 0:
+
+                @pl.when(takes(way, t - 1))
+                def _():
+                    relay(way, t - 1).wait_recv()
+
+            @pl.when(sends(way, t))
+            def _():
+                relay(way, t).start()
+
+        if t == 0:
+            decode(0)
+        elif t == 1:
+            send_tokens(0)
+            decode(1)
+    if ns < 3:
+        send_tokens(0)
+        decode(1)
+    for c in range(1, CHUNKS):
+        send_tokens(c)
+    for way in (1, -1):
+
+        @pl.when(takes(way, ns - 2))
+        def _():
+            relay(way, ns - 2).wait_recv()
 
     load_w.wait()
-    for copy in cot_copies:
-        copy.wait_recv()
-
     @pl.loop(0, CHUNKS)
     def _(c):
         rows_c = pl.ds(pl.multiple_of(c * span, 128), span)
@@ -426,10 +471,11 @@
             grad = red[c, chip, block, :].astype(jnp.float32)
             for k in range(chips - 1):
                 grad = grad + chip_recv[c, k, block, :].astype(jnp.float32)
-            grad = grad * gain_rows[c, block, 0:1]
+            first_gain = shard * rows + c * span + rep * piece + row
+            grad = grad * column(gains, first_gain, 1, 16)[:, 0:1]
             weight = w_v[pl.ds(pl.multiple_of(c * span + rep * piece + row, 16), 16), :]
             new_part, first, second = adam_update(
-                weight, grad, old_m[c, block, :], old_v[c, block, :]
+                weight, grad, old[0, c, block, :], old[1, c, block, :]
             )
             nw_own[c, block, :] = new_part
             place = (
@@ -529,36 +575,15 @@
         for copy in ag_copies[c] + chip_copies[c]:
             copy.wait_send()
         core_copies[c].wait_send()
-    for copy in cot_copies + tok_copies + ng_copies + gain_copies + scale_copies + gz_copies:
+    for t in range(ns - 1):
+        for way in (1, -1):
+
+            @pl.when(sends(way, t))
+            def _():
+                relay(way, t).wait_send()
+
+    for copy in tok_copies + ng_copies + gain_copies + scale_copies + gz_copies:
         copy.wait_send()
-
-
-def decode_rows(codes_m, codes_v, scale_m, scale_v, qmap_m, qmap_v, part, row_group):
-    width = codes_m.shape[1]
-    rows = CHUNKS * part
-
-    def spread(scale):
-        mine = scale.reshape(CHUNKS, -1, part // row_group)
-        mine = lax.dynamic_index_in_dim(mine, lax.axis_index("rep"), 1, keepdims=False)
-        return jnp.broadcast_to(jnp.repeat(mine.reshape(-1), row_group)[:, None], (rows, 128))
-
-    vmem = pl.BlockSpec(memory_space=pltpu.VMEM)
-    anywhere = pl.BlockSpec(memory_space=pl.ANY)
-    shape = jax.ShapeDtypeStruct((rows, width), jnp.float32)
-    chunk_rows = codes_m.shape[0] // CHUNKS
-    return pl.pallas_call(
-        lambda *refs: decode_kernel(CHUNKS, chunk_rows, part, *refs),
-        out_shape=(shape, shape),
-        in_specs=[vmem] * 4 + [anywhere] * 2,
-        out_specs=(vmem, vmem),
-        scratch_shapes=[
-            pltpu.VMEM((rows, width), jnp.int32),
-            pltpu.VMEM((rows, width), jnp.int32),
-            pltpu.SemaphoreType.DMA((2, CHUNKS)),
-        ],
-        compiler_params=pltpu.CompilerParams(vmem_limit_bytes=16 * 2**20),
-        name="decode",
-    )(qmap_m.reshape(2, 128), qmap_v.reshape(2, 128), spread(scale_m), spread(scale_v), codes_m, codes_v)
 
 
 def fused_shards(
@@ -568,16 +593,12 @@
     rows, width = key_weight.shape
     row_group = BLOCK // width
     nr, ns = lax.axis_size("rep"), lax.axis_size("shard")
-    rep, shard = lax.axis_index("rep"), lax.axis_index("shard")
     span = rows // CHUNKS
     part = span // nr
     chips = nr // 2
-    old_m, old_v = decode_rows(codes_m, codes_v, scale_m, scale_v, qmap_m, qmap_v, part, row_group)
-    gains = lax.dynamic_index_in_dim(norm_gain.reshape(ns, CHUNKS, nr, part), shard, 0, False)
-    gains = lax.dynamic_index_in_dim(gains, rep, 1, False)
-    gain_rows = jnp.broadcast_to(gains[:, :, None], (CHUNKS, part, 128))
     vmem = pl.BlockSpec(memory_space=pltpu.VMEM)
     anywhere = pl.BlockSpec(memory_space=pl.ANY)
+    smem = pl.BlockSpec(memory_space=pltpu.SMEM)
     lanes = -(-rows // 1024) * 8
     levels = -(-2 * CHUNKS // 8) * 8
     half, full = jnp.bfloat16, jnp.float32
@@ -590,7 +611,7 @@
             jax.ShapeDtypeStruct((ns, lanes, 128), full),
             jax.ShapeDtypeStruct((nr, levels, 128), full),
         ),
-        in_specs=[anywhere, vmem, vmem, vmem, anywhere, vmem, vmem],
+        in_specs=[anywhere, vmem, vmem, smem] + [anywhere] * 3 + [smem] * 2 + [vmem] * 2,
         out_specs=(vmem, anywhere, vmem, vmem),
         scratch_shapes=[
             pltpu.VMEM((count, features), half),
@@ -611,8 +632,11 @@
             pltpu.VMEM((ns, lanes, 128), full),
             pltpu.VMEM((levels, 128), full),
             pltpu.VMEM((nr, levels, 128), full),
+            pltpu.VMEM((2, CHUNKS, part, width), jnp.int32),
+            pltpu.VMEM((2, CHUNKS, part, width), full),
+            dma((2, CHUNKS)),
             dma((3 + 2 * CHUNKS,)),
-            dma((2, ns - 1)),
+            dma((2, 2, ns - 1)),
             dma((2, CHUNKS, ns - 1)),
             dma((2, ns - 1)),
             dma((2, CHUNKS)),
@@ -634,10 +658,14 @@
         tokens,
         key_cot,
         norm_gain.reshape(1, features),
-        gain_rows,
+        norm_gain,
         key_weight,
-        old_m.reshape(CHUNKS, part, width),
-        old_v.reshape(CHUNKS, part, width),
+        codes_m,
+        codes_v,
+        scale_m,
+        scale_v,
+        qmap_m.reshape(2, 128),
+        qmap_v.reshape(2, 128),
     )
     gain_grad = gain_tiles[:, : rows // 128].reshape(features)
     maxima = scale_tiles[:, : 2 * CHUNKS, : part // row_group]

time: 108 us -> 100 us (0.926)
  the two profiles are of different devices: /device:TPU:15 before, /device:TPU:0 now
where the time goes in v3:
time: 100 us; the launch traced here: 99.8 us
  Pallas kernels  84.3 us (84%)
  local copies, waits for them, and re-layouts  14.8 us (15%)
    pallas_call x1, Pallas kernels, fused_shards(): pl.pallas_call(lambda *refs: fused_kernel(nr, ns, *refs), out_shape=(jax....  84.3 us
    unnamed x20, local copies, waits for them, and re-layouts  9.31 us
    squeeze x2, local copies, waits for them, and re-layouts, fused_shards(): return (input_grad, gain_grad, new_weight, maxima[0], maxima[1])  2.06 us

profile of v3, /device:TPU:0, one launch (start us, length us, event | category | flops | bytes accessed | tf_op | source)
XLA Modules:
  0.0 99.8 jit_solution(3076082215368610600)
XLA Ops:
  0.6 0.7 reshape.30.refs_2_
  1.4 0.0 copy-start
  1.4 1.3 %copy-done = bf16[128,4608]{1,0:T(8,128)(2,1)S(1)} copy-done((bf16[128,4608]{1,0:T(8,128)(2,1)S(1)}, bf16[128,4608]{1,0:T(8,128)(2,1)}, u32[]{:S(2)}) %copy-start) | copy-done | bytes 1179672
  2.7 0.0 copy-start.1
  2.7 0.9 copy-done.1
  3.6 0.0 copy-start.2
  3.6 0.7 copy-done.2
  4.3 0.0 copy-start.5
  4.3 0.7 copy-done.5
  5.0 0.0 copy-start.6
  5.0 0.7 copy-done.6
  5.7 0.0 copy-start.7
  5.7 0.7 copy-done.7
  6.4 0.0 copy-start.8
  6.4 0.7 copy-done.8
  7.1 84.3 %fused.1 = (bf16[128,4608]{1,0:T(8,128)(2,1)S(1)}, bf16[1152,1024]{1,0:T(8,128)(2,1)S(1)}, f32[4,16,128]{2,1,0:T(8,128)S(1)}, f32[8,8,128]{2,1,0:T(8,128)S(1)}) custom-call(bf16[128,4608]{1,0:T(8,128)(2,1)S(1)} %copy-done, bf16[128,1024]{1,0:T(8,128)(2,1)S(1)} %copy-done.1, f32[1,4608]{1,0:T(1,128)S(1)} %reshape.30.refs_2_, f32[4608]{0:T(1024)S(1)} %copy-done.2, ...), custom_call_target="tpu_custom_call" | custom-call | flops 2415919104 | bytes 12582912 | tf_op jit(solution)/shard_map/fused/pallas_call | solution.py:606
  91.4 0.0 copy-start.3
  91.4 0.6 copy-done.3
  92.0 0.0 copy-start.4
  92.0 0.6 copy-done.4
  92.6 1.4 %reshape.33 = f32[4608]{0:T(1024)} reshape(f32[4,9,128]{2,1,0:T(8,128)} %bitcast.16) | data formatting | bytes 36864 | tf_op jit(solution)/shard_map/reshape | solution.py:670
  94.0 0.8 copy.15
  94.8 0.6 fusion
  95.4 1.4 %squeeze.7 = f32[576]{0:T(1024)} reshape(f32[1,3,8,24]{3,2,0,1:T(8,128)} %get-tuple-element.13) | data formatting | bytes 4608 | tf_op jit(solution)/shard_map/squeeze | solution.py:673
  96.7 0.7 squeeze.6
  97.4 1.0 %copy.18 = bf16[128,4608]{1,0:T(8,128)(2,1)} copy(bf16[128,4608]{1,0:T(8,128)(2,1)S(1)} %get-tuple-element.20) | data formatting | bytes 2359296
  98.4 1.4 %copy.19 = bf16[1152,1024]{1,0:T(8,128)(2,1)} copy(bf16[1152,1024]{1,0:T(8,128)(2,1)S(1)} %get-tuple-element.22) | data formatting | bytes 4718592
Async XLA Ops:
  1.4 1.3 %copy-start = (bf16[128,4608]{1,0:T(8,128)(2,1)S(1)}, bf16[128,4608]{1,0:T(8,128)(2,1)}, u32[]{:S(2)}) copy-start(bf16[128,4608]{1,0:T(8,128)(2,1)} %refs_0_.1) | copy-start | bytes 3538948
  2.7 0.9 copy-start.1
  3.6 0.7 copy-start.2
  4.3 0.7 copy-start.5
  5.0 0.7 copy-start.6
  5.7 0.7 copy-start.7
  6.4 0.7 copy-start.8
  91.4 0.6 copy-start.3
  92.0 0.6 copy-start.4

commit v4 on v3

--- a/solution.py
+++ b/solution.py
@@ -274,6 +274,26 @@
             )
         )
         own_tok[c].start()
+    tok_copies = []
+    for c in range(CHUNKS):
+        for k in range(1, ns):
+            col = pl.multiple_of(next_shard(k) * rows + c * span, 128)
+            tok_copies.append(
+                remote(
+                    tok_hbm.at[:, pl.ds(col, span)],
+                    tok_g.at[c, mine],
+                    tok_sem,
+                    (c, k - 1),
+                    shard=next_shard(k),
+                )
+            )
+
+    def send_tokens(c):
+        for k in range(ns - 1):
+            tok_copies[c * (ns - 1) + k].start()
+
+    pl.semaphore_wait(barrier, ns - 1 + nr - 1)
+    send_tokens(0)
     load_tok.wait()
 
     @pl.loop(0, count // 16)
@@ -290,26 +310,6 @@
         scaled = (cot_ref[block, :].astype(jnp.float32) * inv).astype(jnp.bfloat16)
         cot_g[pl.ds(pl.multiple_of(shard * count + row, 16), 16), :] = scaled
 
-    pl.semaphore_wait(barrier, ns - 1 + nr - 1)
-
-    tok_copies = []
-    for c in range(CHUNKS):
-        for k in range(1, ns):
-            col = pl.multiple_of(next_shard(k) * rows + c * span, 128)
-            tok_copies.append(
-                remote(
-                    tok_hbm.at[:, pl.ds(col, span)],
-                    tok_g.at[c, mine],
-                    tok_sem,
-                    (c, k - 1),
-                    shard=next_shard(k),
-                )
-            )
-
-    def send_tokens(c):
-        for k in range(ns - 1):
-            tok_copies[c * (ns - 1) + k].start()
-
     def decode(i):
         table_ref, scale = ((table_m, scale_m), (table_v, scale_v))[i]
         tables = [jnp.broadcast_to(table_ref[k : k + 1, :], (8, 128)) for k in range(2)]
@@ -355,12 +355,12 @@
         if t == 0:
             decode(0)
         elif t == 1:
-            send_tokens(0)
+            send_tokens(1)
             decode(1)
     if ns < 3:
-        send_tokens(0)
+        send_tokens(1)
         decode(1)
-    for c in range(1, CHUNKS):
+    for c in range(2, CHUNKS):
         send_tokens(c)
     for way in (1, -1):
 
@@ -369,24 +369,28 @@
             relay(way, ns - 2).wait_recv()
 
     load_w.wait()
-    @pl.loop(0, CHUNKS)
-    def _(c):
-        rows_c = pl.ds(pl.multiple_of(c * span, 128), span)
+    own_ng = pltpu.make_async_copy(ng.at[:, mine], ng_home.at[shard], loc.at[2 + CHUNKS])
+    ng_copies = []
+    for c in range(CHUNKS):
         ng[c] = lax.dot_general(
             cot_g[...],
-            w_v[rows_c, :],
+            w_v[c * span : (c + 1) * span, :],
             (((1,), (1,)), ((), ())),
             preferred_element_type=jnp.float32,
         ).astype(jnp.bfloat16)
-
-    own_ng = pltpu.make_async_copy(ng.at[:, mine], ng_home.at[shard], loc.at[2 + CHUNKS])
+        for k in range(1, ns):
+            theirs = pl.ds(pl.multiple_of(next_shard(k) * count, count), count)
+            ng_copies.append(
+                remote(
+                    ng.at[c, theirs],
+                    ng_home.at[shard, c],
+                    ng_sem,
+                    (c, k - 1),
+                    shard=next_shard(k),
+                )
+            )
+            ng_copies[-1].start()
     own_ng.start()
-    ng_copies = []
-    for k in range(1, ns):
-        theirs = pl.ds(pl.multiple_of(next_shard(k) * count, count), count)
-        ng_copies.append(
-            remote(ng.at[:, theirs], ng_home.at[shard], ng_sem, (k - 1,), shard=next_shard(k))
-        )
 
     core_copies = [
         remote(part.at[c, :, 1 - core], core_recv.at[c], core_sem, (c,), rep=partner)
@@ -505,8 +509,6 @@
     reduce_core(0)
     form(1)
     reduce_core(1)
-    for copy in ng_copies:
-        copy.start()
     update(0)
     form(2)
     gain_copies = [
@@ -527,20 +529,6 @@
         copy.start()
     scale_recv[rep] = scale_own[...]
     forward(1)
-    total = gain_own[...]
-    for k in range(nr - 1):
-        gain_copies[k].wait_recv()
-        total = total + gain_recv[k]
-    gain_sum[...] = total
-    gz_copies = [
-        remote(gain_sum, gain_z.at[shard], gz_sem, (k - 1,), shard=next_shard(k))
-        for k in range(1, ns)
-    ]
-    for copy in gz_copies:
-        copy.start()
-    gain_z[shard] = total
-    forward(2)
-
     own_ng.wait()
     for copy in ng_copies:
         copy.wait_recv()
@@ -561,6 +549,20 @@
             scaled = ng_home[p, c, block, o : o + 128].astype(jnp.float32) * gain_ref[:, col : col + 128]
             wide = tok_v[block, col : col + 128].astype(jnp.float32)
             ig_ref[block, col : col + 128] = (scaled - wide * factor).astype(jnp.bfloat16)
+
+    total = gain_own[...]
+    for k in range(nr - 1):
+        gain_copies[k].wait_recv()
+        total = total + gain_recv[k]
+    gain_sum[...] = total
+    gz_copies = [
+        remote(gain_sum, gain_z.at[shard], gz_sem, (k - 1,), shard=next_shard(k))
+        for k in range(1, ns)
+    ]
+    for copy in gz_copies:
+        copy.start()
+    gain_z[shard] = total
+    forward(2)
 
     for copy in gz_copies + scale_copies:
         copy.wait_recv()
@@ -638,7 +640,7 @@
             dma((3 + 2 * CHUNKS,)),
             dma((2, 2, ns - 1)),
             dma((2, CHUNKS, ns - 1)),
-            dma((2, ns - 1)),
+            dma((2, CHUNKS, ns - 1)),
             dma((2, CHUNKS)),
             dma((2, CHUNKS, chips - 1)),
             dma((2, CHUNKS, chips)),
@@ -648,7 +650,7 @@
             dma((2, nr - 1)),
         ],
         compiler_params=pltpu.CompilerParams(
-            collective_id=0, has_side_effects=True, vmem_limit_bytes=48 * 2**20
+            collective_id=0, has_side_effects=True, vmem_limit_bytes=60 * 2**20
         ),
         cost_estimate=pl.CostEstimate(
             flops=4 * ns * count * rows * width, bytes_accessed=12 * 2**20, transcendentals=0

time: 100 us -> 93.9 us (0.939)
  local copies, waits for them, and re-layouts: 14.8 us -> 8.76 us
    unnamed x20 -> x4, local copies, waits for them, and re-layouts: 9.31 us -> 3.77 us
where the time goes in v4:
time: 93.9 us; the launch traced here: 93.6 us
  Pallas kernels  84.2 us (90%)
  local copies, waits for them, and re-layouts  8.76 us (9%)
    pallas_call x1, Pallas kernels, fused_shards(): pl.pallas_call(lambda *refs: fused_kernel(nr, ns, *refs), out_shape=(jax....  84.2 us
    unnamed x4, local copies, waits for them, and re-layouts  3.77 us

profile of v4, /device:TPU:0, one launch (start us, length us, event | category | flops | bytes accessed | tf_op | source)
XLA Modules:
  0.0 93.6 jit_solution(14047047058389380677)
XLA Ops:
  0.6 1.3 %reshape.30.refs_2_ = f32[1,4608]{1,0:T(1,128)} reshape(f32[4608]{0:T(1024)} %refs_3_.1) | data formatting | bytes 36864 | tf_op jit(solution)/shard_map/reshape | solution.py:662
  2.0 84.2 %fused.1 = (bf16[128,4608]{1,0:T(8,128)(2,1)}, bf16[1152,1024]{1,0:T(8,128)(2,1)}, f32[4,16,128]{2,1,0:T(8,128)}, f32[8,8,128]{2,1,0:T(8,128)}) custom-call(bf16[128,4608]{1,0:T(8,128)(2,1)} %refs_0_.1, bf16[128,1024]{1,0:T(8,128)(2,1)} %refs_1_.1, f32[1,4608]{1,0:T(1,128)} %reshape.30.refs_2_, f32[4608]{0:T(1024)} %refs_3_.1, bf16[1152,1024]{1,0:T(8,128)(2,1)} %refs_4_.1, ...), custom_call_target="tpu_custom_call" | custom-call | flops 2415919104 | bytes 12582912 | tf_op jit(solution)/shard_map/fused/pallas_call | solution.py:608
  86.1 0.0 copy-start
  86.2 1.5 %reshape.33 = f32[4608]{0:T(1024)} reshape(f32[4,9,128]{2,1,0:T(8,128)} %bitcast.17) | data formatting | bytes 36864 | tf_op jit(solution)/shard_map/reshape | solution.py:672
  87.7 0.8 copy.15
  88.4 0.7 squeeze.7
  89.1 0.7 squeeze.6
  89.8 2.4 %copy.18 = bf16[128,4608]{1,0:T(8,128)(2,1)} copy(bf16[128,4608]{1,0:T(8,128)(2,1)} %get-tuple-element.20) | data formatting | bytes 2359296
  92.2 0.0 copy-done
  92.2 1.4 %copy.19 = bf16[1152,1024]{1,0:T(8,128)(2,1)} copy(bf16[1152,1024]{1,0:T(8,128)(2,1)S(1)} %copy-done) | data formatting | bytes 4718592
  (1 shorter events, 0.0 us)
Async XLA Ops:
  86.1 6.0 %copy-start = (bf16[1152,1024]{1,0:T(8,128)(2,1)S(1)}, bf16[1152,1024]{1,0:T(8,128)(2,1)}, u32[]{:S(2)}) copy-start(bf16[1152,1024]{1,0:T(8,128)(2,1)} %get-tuple-element.22) | copy-start | bytes 7077892
